TPU v7x, 512 devices: a whole 4x4x16 slice. The times are simulated.
512 devices in a mesh: ctx: 32 (over y, x, core), tp: 16 (over z).
Axes of the slice: x: 4, y: 4, z: 16, core: 2. Of those that a mesh axis runs over, the one named last changes fastest.
Arguments:
- features: bfloat16 [8192, 3, 4096], P('ctx', None, 'tp'), may hold values from -6 to 6
- short_taps: float32 [3, 3, 4096], P(None, None, 'tp'), may hold values from -3.5 to 3.5
- residues: float32 [16, 256], P(None, 'tp'), may hold values from -1.5 to 1.5
- rates: float32 [16, 256], P(None, 'tp'), may hold values from 3.6621094e-05 to 0.05, as said below
- skip: float32 [4096], P('tp'), may hold values from -4 to 4
- out_weight: bfloat16 [4096, 4096], P(None, 'tp'), may hold values from -0.09375 to 0.09375
Outputs:
- mixed: bfloat16 [8192, 4096], P('ctx', 'tp')
Inputs may be any that keep to these rules, and one draw needn't show every extreme that they name: `rates`: decay rate of one mode of one filter.
All inputs are finite; a program needn't handle non-finite values.
Results may differ from a plain program's by a relative error of at most 0.0049.
Values may be sent and summed in bfloat16 or wider, within the bound.
No kernel may reach another device: no remote copies, remote signals or barrier semaphores. Data moves between devices by JAX's collectives and lax.ppermute only.
A program may use at most 128 MiB of HBM per device.

v0:
```python
import math
import jax
import jax.numpy as jnp
from jax import lax
from jax.sharding import PartitionSpec as P

SHORT = 3


def passed_along(array, axis, by):
    count = lax.axis_size(axis)
    pairs = [(i, i + by) for i in range(count) if 0 <= i + by < count]
    return lax.ppermute(array, axis, pairs)


def regroup(block):
    return lax.all_to_all(block, "ctx", split_axis=0, concat_axis=0, tiled=True)


def mixdot(form, left, right):
    return jnp.einsum(form, left, right, precision=lax.Precision.HIGHEST)


def rotate(real_part, imag_part, cosine, sine, sign):
    return (
        real_part * cosine - sign * imag_part * sine,
        imag_part * cosine + sign * real_part * sine,
    )


def phase_table(numer, denom):
    angle = 2.0 * math.pi / denom * numer.astype(jnp.float32)
    return (jnp.cos(angle), jnp.sin(angle))


def filter_spectrum(residues, rates, own, rows, ctx_count):
    twice = 2 * ctx_count
    seq_len = rows * ctx_count
    total_len = 2 * seq_len
    sub_index = jnp.arange(2, dtype=jnp.int32)[:, None]
    freq_index = jnp.arange(rows, dtype=jnp.int32)[None, :]
    wave = 2 * own + sub_index + twice * freq_index
    signed = jnp.where(wave < seq_len, wave, wave - total_len)
    theta = 2.0 * math.pi / total_len * signed.astype(jnp.float32)
    theta = theta[None, :, :, None]
    decay = rates[:, None, None, :]
    damping = jnp.exp(-decay)
    den_real = -jnp.expm1(-decay) + damping * 2.0 * jnp.sin(0.5 * theta) ** 2
    den_imag = damping * jnp.sin(theta)
    parity = (1 - 2 * sub_index).astype(jnp.float32)[None, :, :, None]
    numer = 1.0 - jnp.exp(-decay * float(seq_len)) * parity
    scaled = (
        residues[:, None, None, :]
        * jnp.sqrt(2.0 * decay)
        * numer
        / (den_real * den_real + den_imag * den_imag)
    )
    return (jnp.sum(scaled * den_real, axis=0), -jnp.sum(scaled * den_imag, axis=0))


def transform_conv(product, residues, rates, ctx_count, own):
    rows = product.shape[0]
    width = product.shape[1]
    filters = residues.shape[1]
    piece = rows // ctx_count
    twice = 2 * ctx_count
    total_len = 2 * rows * ctx_count
    dev_index = jnp.arange(ctx_count, dtype=jnp.int32)
    freq_group = jnp.arange(twice, dtype=jnp.int32)
    cos_outer, sin_outer = phase_table(freq_group[:, None] * dev_index[None, :] % twice, twice)
    local_pos = own * piece + jnp.arange(piece, dtype=jnp.int32)
    cos_twist, sin_twist = phase_table(
        freq_group[:, None] * local_pos[None, :] % total_len, total_len
    )
    cos_twist = cos_twist[:, :, None]
    sin_twist = sin_twist[:, :, None]
    row_index = jnp.arange(rows, dtype=jnp.int32)
    cos_inner, sin_inner = phase_table(row_index[:, None] * row_index[None, :] % rows, rows)
    cos_inner = cos_inner.reshape(rows, ctx_count, piece)
    sin_inner = sin_inner.reshape(rows, ctx_count, piece)
    moved = regroup(product.reshape(ctx_count, piece, width))
    spec_real = mixdot("ca,ajm->cjm", cos_outer, moved)
    spec_imag = -mixdot("ca,ajm->cjm", sin_outer, moved)
    spec_real, spec_imag = rotate(spec_real, spec_imag, cos_twist, sin_twist, -1.0)
    outgoing = jnp.concatenate([spec_real, spec_imag], -1).reshape(ctx_count, 2 * piece, 2 * width)
    arrived = regroup(outgoing).reshape(ctx_count, 2, piece, 2 * width)
    arr_real = arrived[..., :width]
    arr_imag = arrived[..., width:]
    freq_real = mixdot("usj,scjm->cum", cos_inner, arr_real) + mixdot(
        "usj,scjm->cum", sin_inner, arr_imag
    )
    freq_imag = mixdot("usj,scjm->cum", cos_inner, arr_imag) - mixdot(
        "usj,scjm->cum", sin_inner, arr_real
    )
    filt_real, filt_imag = filter_spectrum(residues, rates, own, rows, ctx_count)
    filt_real = filt_real[..., None]
    filt_imag = filt_imag[..., None]
    freq_real = freq_real.reshape(2, rows, filters, width // filters)
    freq_imag = freq_imag.reshape(2, rows, filters, width // filters)
    prod_real = (freq_real * filt_real - freq_imag * filt_imag).reshape(2, rows, width)
    prod_imag = (freq_real * filt_imag + freq_imag * filt_real).reshape(2, rows, width)
    back_real = mixdot("usj,cum->scjm", cos_inner, prod_real) - mixdot(
        "usj,cum->scjm", sin_inner, prod_imag
    )
    back_imag = mixdot("usj,cum->scjm", sin_inner, prod_real) + mixdot(
        "usj,cum->scjm", cos_inner, prod_imag
    )
    returning = jnp.concatenate([back_real, back_imag], -1).reshape(ctx_count, 2 * piece, 2 * width)
    returned = regroup(returning).reshape(twice, piece, 2 * width)
    ret_real, ret_imag = rotate(
        returned[..., :width], returned[..., width:], cos_twist, sin_twist, 1.0
    )
    scale = 1.0 / total_len
    out_real = mixdot("ca,cjm->ajm", cos_outer, ret_real) - mixdot(
        "ca,cjm->ajm", sin_outer, ret_imag
    )
    time_rows = out_real * scale
    conv = regroup(time_rows).reshape(rows, width)
    return conv


def shards(features, short_taps, residues, rates, skip, out_weight):
    ctx_count = lax.axis_size("ctx")
    own = lax.axis_index("ctx")
    rows = features.shape[0]
    rim = passed_along(features[rows - (SHORT - 1) :], "ctx", 1)
    extended = jnp.concatenate([rim, features], 0)
    shorted = jnp.zeros(features.shape, jnp.float32)
    for shift in range(SHORT):
        window = extended[SHORT - 1 - shift : SHORT - 1 - shift + rows].astype(jnp.float32)
        shorted = shorted + short_taps[shift] * window
    query = shorted[:, 0, :]
    product = shorted[:, 1, :] * shorted[:, 2, :]
    conv = transform_conv(product, residues, rates, ctx_count, own)
    gated = (query * (conv + skip * product)).astype(jnp.bfloat16)
    projected = jnp.dot(
        lax.all_gather(gated, "tp", axis=1, tiled=True),
        out_weight,
        preferred_element_type=jnp.float32,
    )
    return projected.astype(jnp.bfloat16)


def solution(mesh):
    in_specs = (
        P("ctx", None, "tp"),
        P(None, None, "tp"),
        P(None, "tp"),
        P(None, "tp"),
        P("tp"),
        P(None, "tp"),
    )
    out_specs = P("ctx", "tp")
    return jax.shard_map(shards, mesh=mesh, in_specs=in_specs, out_specs=out_specs, check_vma=False)
```

profile of v0, /device:TPU:32, one launch (start us, length us, event | category | flops | bytes accessed | tf_op | source)
XLA Modules:
  0.0 198.4 jit_solution(7042605041022296858)
XLA Ops:
  6.5 0.9 slice.41
  7.4 1.7 collective-permute-start
  9.9 1.8 multiply_add_fusion
  12.5 9.7 %all-to-all-start = ((f32[32,8,256]{2,1,0:T(8,128)}), f32[32,8,256]{2,1,0:T(8,128)S(1)}, u32[]{:S(2)}, u32[]{:S(2)}) async-start(f32[32,8,256]{2,1,0:T(8,128)} %fusion.68), calls=%async_computation | async-start | bytes 524288 | tf_op jit(solution)/shard_map/all_to_all | solution.py:17
  22.3 8.8 %all-to-all-done = f32[32,8,256]{2,1,0:T(8,128)S(1)} async-done(((f32[32,8,256]{2,1,0:T(8,128)}), f32[32,8,256]{2,1,0:T(8,128)S(1)}, u32[]{:S(2)}, u32[]{:S(2)}) %all-to-all-start) | async-done | bytes 262176 | tf_op jit(solution)/shard_map/all_to_all | solution.py:17
  31.8 0.8 multiply_subtract_fusion
  32.8 1.6 copy.36
  34.4 4.7 %all-to-all-start.1 = ((f32[32,16,512]{2,1,0:T(8,128)}), f32[32,16,512]{2,1,0:T(8,128)}, u32[]{:S(2)}, u32[]{:S(2)}) async-start(f32[32,16,512]{2,1,0:T(8,128)} %bitcast.118), calls=%async_computation.1 | async-start | bytes 2097152 | tf_op jit(solution)/shard_map/all_to_all | solution.py:17
  39.9 16.5 %all-to-all-done.1 = f32[32,16,512]{2,1,0:T(8,128)} async-done(((f32[32,16,512]{2,1,0:T(8,128)}), f32[32,16,512]{2,1,0:T(8,128)}, u32[]{:S(2)}, u32[]{:S(2)}) %all-to-all-start.1) | async-done | bytes 1048608 | tf_op jit(solution)/shard_map/all_to_all | solution.py:17
  56.4 1.8 copy.37
  58.2 1.9 convolution_bitcast_fusion.2
  60.1 1.9 convolution_bitcast_fusion
  62.0 1.9 fusion.3
  63.9 1.9 fusion.11
  65.9 1.6 fusion.14
  67.5 1.8 fusion.16
  69.3 1.6 fusion
  70.9 1.6 fusion.1
  73.2 20.6 %all_to_all.20 = f32[32,16,512]{2,1,0:T(8,128)S(1)} all-to-all(f32[32,16,512]{2,1,0:T(8,128)S(1)} %copy.42), channel_id=1, replica_groups=mesh['ctx'=32,'tp'=16] {'ctx'}, dimensions={0} | all-to-all | bytes 2097152 | tf_op jit(solution)/shard_map/all_to_all | solution.py:17
  94.0 0.8 fusion.21
  94.7 0.8 fusion.6
  95.7 12.3 %all_to_all.21 = f32[32,8,256]{2,1,0:T(8,128)S(1)} all-to-all(f32[32,8,256]{2,1,0:T(8,128)S(1)} %copy.45), channel_id=1, replica_groups=mesh['ctx'=32,'tp'=16] {'ctx'}, dimensions={0} | all-to-all | bytes 524288 | tf_op jit(solution)/shard_map/all_to_all | solution.py:17
  108.7 79.9 %all-gather.2.cloned.1.call-done = bf16[256,4096]{1,0:T(8,128)(2,1)} async-done(((bf16[256,256]{1,0:T(8,128)(2,1)}), bf16[256,4096]{1,0:T(8,128)(2,1)}) %all-gather.2.cloned.1.call-update) | async-done | bytes 2097168 | tf_op jit(solution)/shard_map/all_gather | solution.py:137
  188.6 3.0 %convolution_convert_fusion = bf16[256,256]{1,0:T(8,128)(2,1)} fusion(bf16[256,4096]{1,0:T(8,128)(2,1)} %all-gather.2.cloned.1.call-done, bf16[4096,256]{1,0:T(8,128)(2,1)S(1)} %copy-done), kind=kOutput, calls=%fused_computation.15 | convolution fusion | flops 536936448 | bytes 4325376 | tf_op jit(solution)/shard_map/dot_general | solution.py:136
  (31 shorter events, 5.0 us)
Async XLA Ops:
  6.5 182.0 %copy-start = (bf16[4096,256]{1,0:T(8,128)(2,1)S(1)}, bf16[4096,256]{1,0:T(8,128)(2,1)}, u32[]{:S(2)}) copy-start(bf16[4096,256]{1,0:T(8,128)(2,1)} %param.11) | copy-start | bytes 6291460
  7.4 2.5 %collective-permute-start = (bf16[2,3,256]{2,0,1:T(2,128)(2,1)S(1)}, bf16[2,3,256]{2,0,1:T(2,128)(2,1)S(1)}, u32[]{:S(2)}, u32[]{:S(2)}) collective-permute-start(bf16[2,3,256]{2,0,1:T(2,128)(2,1)S(1)} %slice.41), channel_id=1, source_target_pairs={{0,16},{16,32},{32,48},{48,64},{64,80},{80,96},{96,112},{112,128},... | collective-permute-start | bytes 9224 | tf_op jit(solution)/shard_map/ppermute | solution.py:13
  12.5 18.6 %all-to-all-start = ((f32[32,8,256]{2,1,0:T(8,128)}), f32[32,8,256]{2,1,0:T(8,128)S(1)}, u32[]{:S(2)}, u32[]{:S(2)}) async-start(f32[32,8,256]{2,1,0:T(8,128)} %fusion.68), calls=%async_computation | async-start | bytes 524288 | tf_op jit(solution)/shard_map/all_to_all | solution.py:17
  32.8 6.7 %copy-start.1 = (f32[16,16]{1,0:T(8,128)S(1)}, f32[16,16]{1,0:T(8,128)}, u32[]{:S(2)}) copy-start(f32[16,16]{1,0:T(8,128)} %param.8) | copy-start | bytes 3076
  32.8 6.7 %copy-start.2 = (f32[16,16]{1,0:T(8,128)S(1)}, f32[16,16]{1,0:T(8,128)}, u32[]{:S(2)}) copy-start(f32[16,16]{1,0:T(8,128)} %param.9) | copy-start | bytes 3076
  34.4 22.0 %all-to-all-start.1 = ((f32[32,16,512]{2,1,0:T(8,128)}), f32[32,16,512]{2,1,0:T(8,128)}, u32[]{:S(2)}, u32[]{:S(2)}) async-start(f32[32,16,512]{2,1,0:T(8,128)} %bitcast.118), calls=%async_computation.1 | async-start | bytes 2097152 | tf_op jit(solution)/shard_map/all_to_all | solution.py:17
  39.1 149.5 %all-gather.2.cloned.1.call-start = ((), (), s32[]{:S(2)}) async-start(), calls=%async_computation.4 | async-start | bytes 2228224 | tf_op jit(solution)/shard_map/all_gather | solution.py:137
  94.0 14.0 %copy-start.3 = (f32[256]{0:T(256)S(1)}, f32[256]{0:T(256)}, u32[]{:S(2)}) copy-start(f32[256]{0:T(256)} %param.10) | copy-start | bytes 3076
Sparse Core Ops, SparseCore 0:
  108.8 79.7 all-gather.1
where the time goes:
time: 199 us; the launch traced here: 198 us
  waiting for transfers between devices  105 us (53%)
  blocking collectives  32.9 us (17%)
  matrix products  20.2 us (10%)
  starting transfers between devices  16.3 us (8%)
  between operations  13.7 us (7%)
  local copies, waits for them, and re-layouts  5.9 us (3%)
  other arithmetic  4.2 us (2%)
    all_gather x1, waiting for transfers between devices, shards(): lax.all_gather(gated, 'tp', axis=1, tiled=True)  79.9 us
    all_to_all x2, blocking collectives, regroup(): return lax.all_to_all(block, 'ctx', split_axis=0, concat_axis=0, tiled=True)  32.9 us
    all_to_all x2, waiting for transfers between devices, regroup(): return lax.all_to_all(block, 'ctx', split_axis=0, concat_axis=0, tiled=True)  25.2 us
    dot_general x12, matrix products, mixdot(): return jnp.einsum(form, left, right, precision=lax.Precision.HIGHEST)  17.2 us
    all_to_all x2, starting transfers between devices, regroup(): return lax.all_to_all(block, 'ctx', split_axis=0, concat_axis=0, tiled=True)  14.4 us
  transfers between devices with their start and end apart: 4, of which 4 were waited for; matrix products, arithmetic and copies ran while one was open for 1% of the time, Pallas kernels for 0%

commit v1 on v0

--- a/solution.py
+++ b/solution.py
@@ -5,6 +5,14 @@
 from jax.sharding import PartitionSpec as P
 
 SHORT = 3
+
+
+def gather_from_all(array, axis, dim):
+    size = lax.axis_size(axis)
+    repeats = [size if d == dim else 1 for d in range(array.ndim)]
+    return lax.all_to_all(
+        jnp.tile(array, repeats), axis, split_axis=dim, concat_axis=dim, tiled=True
+    )
 
 
 def passed_along(array, axis, by):
@@ -134,9 +142,7 @@
     conv = transform_conv(product, residues, rates, ctx_count, own)
     gated = (query * (conv + skip * product)).astype(jnp.bfloat16)
     projected = jnp.dot(
-        lax.all_gather(gated, "tp", axis=1, tiled=True),
-        out_weight,
-        preferred_element_type=jnp.float32,
+        gather_from_all(gated, "tp", 1), out_weight, preferred_element_type=jnp.float32
     )
     return projected.astype(jnp.bfloat16)
 

time: 199 us -> 221 us (1.11)
  blocking collectives: 32.9 us -> 145 us
  waiting for transfers between devices: 105 us -> 25.4 us
  between operations: 13.7 us -> 0.28 us
  local copies, waits for them, and re-layouts: 5.9 us -> 10 us
    all_to_all x0 -> x1, blocking collectives: none -> 112 us  [gather_from_all(): lax.all_to_all(jnp.tile(array, repeats), axis, split_axis=dim, concat_axi...]
    all_gather x1 -> x0, waiting for transfers between devices: 79.9 us -> none  [shards(): lax.all_gather(gated, 'tp', axis=1, tiled=True)]
    all_to_all x0 -> x1, local copies, waits for them, and re-layouts: none -> 3.91 us  [gather_from_all(): lax.all_to_all(jnp.tile(array, repeats), axis, split_axis=dim, concat_axi...]
  transfers between devices with their start and end apart: 4 -> 3, of which waited for: 4 -> 3; matrix products, arithmetic and copies ran while one was open for 1% -> 1% of each run, Pallas kernels for 0% -> 0%
where the time goes in v1:
time: 221 us
  blocking collectives  145 us (66%)
  waiting for transfers between devices  25.4 us (11%)
  matrix products  20.2 us (9%)
  starting transfers between devices  16.3 us (7%)
  local copies, waits for them, and re-layouts  10 us (5%)
  other arithmetic  3.41 us (2%)
    all_to_all x1, blocking collectives, gather_from_all(): lax.all_to_all(jnp.tile(array, repeats), axis, split_axis=dim, concat_axi...  112 us
    all_to_all x2, blocking collectives, regroup(): return lax.all_to_all(block, 'ctx', split_axis=0, concat_axis=0, tiled=True)  32.9 us
    all_to_all x2, waiting for transfers between devices, regroup(): return lax.all_to_all(block, 'ctx', split_axis=0, concat_axis=0, tiled=True)  25.3 us
    dot_general x12, matrix products, mixdot(): return jnp.einsum(form, left, right, precision=lax.Precision.HIGHEST)  17.2 us
    all_to_all x2, starting transfers between devices, regroup(): return lax.all_to_all(block, 'ctx', split_axis=0, concat_axis=0, tiled=True)  14.5 us
  transfers between devices with their start and end apart: 3, of which 3 were waited for; matrix products, arithmetic and copies ran while one was open for 1% of the time, Pallas kernels for 0%

profile of v1, /device:TPU:32, one launch (start us, length us, event | category | flops | bytes accessed | tf_op | source)
XLA Modules:
  0.0 220.7 jit_solution(3040311563817707789)
XLA Ops:
  0.0 0.9 slice.41
  0.9 1.7 collective-permute-start
  3.4 1.7 multiply_add_fusion
  5.8 9.7 %all-to-all-start = ((f32[32,8,256]{2,1,0:T(8,128)}), f32[32,8,256]{2,1,0:T(8,128)S(1)}, u32[]{:S(2)}, u32[]{:S(2)}) async-start(f32[32,8,256]{2,1,0:T(8,128)} %fusion.68), calls=%async_computation | async-start | bytes 524288 | tf_op jit(solution)/shard_map/all_to_all | solution.py:25
  15.7 8.8 %all-to-all-done = f32[32,8,256]{2,1,0:T(8,128)S(1)} async-done(((f32[32,8,256]{2,1,0:T(8,128)}), f32[32,8,256]{2,1,0:T(8,128)S(1)}, u32[]{:S(2)}, u32[]{:S(2)}) %all-to-all-start) | async-done | bytes 262176 | tf_op jit(solution)/shard_map/all_to_all | solution.py:25
  25.1 0.8 multiply_subtract_fusion
  26.1 1.6 copy.49
  27.7 4.8 %all-to-all-start.1 = ((f32[32,16,512]{2,1,0:T(8,128)}), f32[32,16,512]{2,1,0:T(8,128)}, u32[]{:S(2)}, u32[]{:S(2)}) async-start(f32[32,16,512]{2,1,0:T(8,128)} %bitcast.119), calls=%async_computation.1 | async-start | bytes 2097152 | tf_op jit(solution)/shard_map/all_to_all | solution.py:25
  33.2 16.5 %all-to-all-done.1 = f32[32,16,512]{2,1,0:T(8,128)} async-done(((f32[32,16,512]{2,1,0:T(8,128)}), f32[32,16,512]{2,1,0:T(8,128)}, u32[]{:S(2)}, u32[]{:S(2)}) %all-to-all-start.1) | async-done | bytes 1048608 | tf_op jit(solution)/shard_map/all_to_all | solution.py:25
  49.7 1.8 copy.50
  51.6 1.9 convolution_bitcast_fusion
  53.5 1.9 convolution_bitcast_fusion.2
  55.4 1.9 fusion.3
  57.3 1.9 fusion.11
  59.2 1.6 fusion.14
  60.8 1.8 fusion.16
  62.6 1.6 fusion.1
  64.2 1.6 fusion
  66.6 20.6 %all_to_all.29 = f32[32,16,512]{2,1,0:T(8,128)S(1)} all-to-all(f32[32,16,512]{2,1,0:T(8,128)S(1)} %copy.55), channel_id=1, replica_groups=mesh['ctx'=32,'tp'=16] {'ctx'}, dimensions={0} | all-to-all | bytes 2097152 | tf_op jit(solution)/shard_map/all_to_all | solution.py:25
  87.3 0.8 fusion.21
  89.0 12.3 %all_to_all.30 = f32[32,8,256]{2,1,0:T(8,128)S(1)} all-to-all(f32[32,8,256]{2,1,0:T(8,128)S(1)} %copy.58), channel_id=1, replica_groups=mesh['ctx'=32,'tp'=16] {'ctx'}, dimensions={0} | all-to-all | bytes 524288 | tf_op jit(solution)/shard_map/all_to_all | solution.py:25
  101.5 112.2 %all_to_all.31 = bf16[256,16,256]{2,0,1:T(8,128)(2,1)} all-to-all(bf16[256,16,256]{2,0,1:T(8,128)(2,1)S(1)} %tile.2), channel_id=1, replica_groups=mesh['ctx'=32,'tp'=16] {'tp'}, dimensions={1} | all-to-all | bytes 4194304 | tf_op jit(solution)/shard_map/all_to_all | solution.py:13
  213.8 3.9 %copy.59 = bf16[256,16,256]{0,2,1:T(8,128)(2,1)} copy(bf16[256,16,256]{2,0,1:T(8,128)(2,1)} %all_to_all.31) | data formatting | bytes 4194304 | tf_op jit(solution)/shard_map/all_to_all | solution.py:13
  217.7 3.0 %convolution_convert_fusion = bf16[256,256]{1,0:T(8,128)(2,1)} fusion(bf16[256,4096]{0,1:T(8,128)(2,1)} %bitcast.126, bf16[4096,256]{1,0:T(8,128)(2,1)S(1)} %copy-done), kind=kOutput, calls=%fused_computation.15 | convolution fusion | flops 536936448 | bytes 4325376 | tf_op jit(solution)/shard_map/dot_general | solution.py:144
  (31 shorter events, 5.0 us)
Async XLA Ops:
  0.0 217.7 %copy-start = (bf16[4096,256]{1,0:T(8,128)(2,1)S(1)}, bf16[4096,256]{1,0:T(8,128)(2,1)}, u32[]{:S(2)}) copy-start(bf16[4096,256]{1,0:T(8,128)(2,1)} %param.11) | copy-start | bytes 6291460
  0.9 2.5 %collective-permute-start = (bf16[2,3,256]{2,0,1:T(2,128)(2,1)S(1)}, bf16[2,3,256]{2,0,1:T(2,128)(2,1)S(1)}, u32[]{:S(2)}, u32[]{:S(2)}) collective-permute-start(bf16[2,3,256]{2,0,1:T(2,128)(2,1)S(1)} %slice.41), channel_id=1, source_target_pairs={{0,16},{16,32},{32,48},{48,64},{64,80},{80,96},{96,112},{112,128},... | collective-permute-start | bytes 9224 | tf_op jit(solution)/shard_map/ppermute | solution.py:21
  5.8 18.6 %all-to-all-start = ((f32[32,8,256]{2,1,0:T(8,128)}), f32[32,8,256]{2,1,0:T(8,128)S(1)}, u32[]{:S(2)}, u32[]{:S(2)}) async-start(f32[32,8,256]{2,1,0:T(8,128)} %fusion.68), calls=%async_computation | async-start | bytes 524288 | tf_op jit(solution)/shard_map/all_to_all | solution.py:25
  26.1 6.6 %copy-start.1 = (f32[16,16]{1,0:T(8,128)S(1)}, f32[16,16]{1,0:T(8,128)}, u32[]{:S(2)}) copy-start(f32[16,16]{1,0:T(8,128)} %param.8) | copy-start | bytes 3076
  26.1 6.6 %copy-start.2 = (f32[16,16]{1,0:T(8,128)S(1)}, f32[16,16]{1,0:T(8,128)}, u32[]{:S(2)}) copy-start(f32[16,16]{1,0:T(8,128)} %param.9) | copy-start | bytes 3076
  27.7 22.0 %all-to-all-start.1 = ((f32[32,16,512]{2,1,0:T(8,128)}), f32[32,16,512]{2,1,0:T(8,128)}, u32[]{:S(2)}, u32[]{:S(2)}) async-start(f32[32,16,512]{2,1,0:T(8,128)} %bitcast.119), calls=%async_computation.1 | async-start | bytes 2097152 | tf_op jit(solution)/shard_map/all_to_all | solution.py:25
  87.3 14.0 %copy-start.3 = (f32[256]{0:T(256)S(1)}, f32[256]{0:T(256)}, u32[]{:S(2)}) copy-start(f32[256]{0:T(256)} %param.10) | copy-start | bytes 3076
